TPU v7x, 32 devices: a whole 2x2x4 slice. The times are simulated.
32 devices in a mesh: req: 8 (over y, x, core), blk: 4 (over z).
Axes of the slice: x: 2, y: 2, z: 4, core: 2. Of those that a mesh axis runs over, the one named last changes fastest.
Arguments:
- x_img: bfloat16 [8, 1024, 1536], P('req', 'blk'), may hold values from -0.3 to 0.3
- x_txt: bfloat16 [8, 154, 1536], P('req'), may hold values from -6 to 6
- modulation: float32 [8, 7, 1536], P('req'), may hold values from -8 to 8
- w_img: bfloat16 [1536, 2304], P(None, 'req'), may hold values from -0.375 to 0.375
- w_txt: bfloat16 [1536, 1536], P(None, 'req'), may hold values from -0.15625 to 0.15625
- w_out: bfloat16 [768, 1536], P('req'), may hold values from -0.21875 to 0.21875
- w_final: bfloat16 [1536, 64], replicated, may hold values from -0.15625 to 0.15625
- lengths: int32 [8], P('req'), may hold values from 16 to 154, as said below
- block_mask: int32 [8, 4, 4], P('req', 'blk'), may hold values from 0 to 1, as said below
- timestep: int32 [8], P('req'), may hold values from 0 to 27
- latent: float32 [8, 16, 32, 128], P('req', None, 'blk'), may hold values from -6 to 6
- conv_w: bfloat16 [512, 144], replicated, may hold values from -0.5 to 0.5
Outputs:
- velocity: float32 [8, 16, 32, 128], P('req', None, 'blk')
- latent_next: float32 [8, 16, 32, 128], P('req', None, 'blk')
- features: bfloat16 [8, 512, 32, 128], P('req', None, 'blk')
Inputs may be any that keep to these rules, and one draw needn't show every extreme that they name: Text keys from position lengths[r] on are padding; some request uses all 154 text tokens. Every tile may attend to its own keys: block_mask[r, t, t] = 1.
All inputs are finite; a program needn't handle non-finite values.
Results may differ from a plain program's by a relative error of at most 0.0063.
Values may be sent and summed in bfloat16 or wider, within the bound.
A program may use at most 192 MiB of HBM per device.

v0:
```python
import jax
import jax.numpy as jnp
from jax import lax
from jax.sharding import PartitionSpec as P

HD = 64
GRIDW = 64
PATCH = 2
LATC = 16
NSTEPS = 28
NORM_EPS = 1e-06
SHIFT_FACTOR = 3.0
LATENT_SCALE = 1.5305
LATENT_SHIFT = 0.0609
NEG_LARGE = -1e30
SCORE_SCALE = 0.125


def with_halo(block, sides, width):
    for axis, dim in sides:
        count = lax.axis_size(axis)
        forward = [(i, i + 1) for i in range(count - 1)]
        backward = [(target, source) for source, target in forward]
        low = lax.ppermute(
            lax.slice_in_dim(block, block.shape[dim] - width, None, axis=dim), axis, forward
        )
        high = lax.ppermute(lax.slice_in_dim(block, 0, width, axis=dim), axis, backward)
        block = jnp.concatenate([low, block, high], axis=dim)
    return block


def layer_norm(values):
    values = values.astype(jnp.float32)
    center = values - jnp.mean(values, axis=-1, keepdims=True)
    spread = jnp.mean(center * center, axis=-1, keepdims=True)
    return center * lax.rsqrt(spread + NORM_EPS)


def modulate(values, shift_row, scale_row):
    return layer_norm(values) * (1.0 + scale_row) + shift_row


def sigma_of(step_index, step_count):
    fraction = 1.0 - step_index.astype(jnp.float32) / step_count
    return SHIFT_FACTOR * fraction / (1.0 + (SHIFT_FACTOR - 1.0) * fraction)


def unpatchify(token_out, grid_width, patch_size, channels):
    patch_rows = token_out.shape[0] // grid_width
    shaped = token_out.reshape(patch_rows, grid_width, patch_size, patch_size, channels)
    shaped = jnp.transpose(shaped, (4, 0, 2, 1, 3))
    return shaped.reshape(channels, patch_rows * patch_size, grid_width * patch_size)


def convolve(padded, conv_w):
    row_count = padded.shape[1] - 2
    col_count = padded.shape[2] - 2
    tap_list = [
        padded[:, tap_row : tap_row + row_count, tap_col : tap_col + col_count]
        for tap_row in range(3)
        for tap_col in range(3)
    ]
    stacked = jnp.stack(tap_list, axis=1).reshape(padded.shape[0] * 9, row_count * col_count)
    convolved = jnp.dot(conv_w, stacked, preferred_element_type=jnp.float32)
    return convolved.reshape(conv_w.shape[0], row_count, col_count)


def text_state(queries, keys_txt, vals_txt, length):
    text_allowed = (jnp.arange(keys_txt.shape[0], dtype=jnp.int32) < length)[None, None, :]
    text_scores = (
        jnp.einsum("qhd,khd->qhk", queries, keys_txt, preferred_element_type=jnp.float32)
        * SCORE_SCALE
    )
    text_scores = jnp.where(text_allowed, text_scores, NEG_LARGE)
    text_max = jnp.max(text_scores, axis=2)
    text_weights = jnp.where(text_allowed, jnp.exp(text_scores - text_max[:, :, None]), 0.0)
    text_acc = jnp.einsum(
        "qhk,khd->qhd",
        text_weights.astype(jnp.bfloat16),
        vals_txt,
        preferred_element_type=jnp.float32,
    )
    return (text_max, jnp.sum(text_weights, axis=2), text_acc)


def absorb_block(previous, queries, head_keys, head_vals, allowed):
    old_max, old_sum, old_acc = previous
    scores = (
        jnp.einsum("qhd,khd->qhk", queries, head_keys, preferred_element_type=jnp.float32)
        * SCORE_SCALE
    )
    scores = jnp.where(allowed, scores, NEG_LARGE)
    new_max = jnp.maximum(old_max, jnp.max(scores, axis=2))
    weights = jnp.where(allowed, jnp.exp(scores - new_max[:, :, None]), 0.0)
    factor = jnp.exp(old_max - new_max)
    summed = jnp.einsum(
        "qhk,khd->qhd", weights.astype(jnp.bfloat16), head_vals, preferred_element_type=jnp.float32
    )
    return (
        new_max,
        old_sum * factor + jnp.sum(weights, axis=2),
        old_acc * factor[:, :, None] + summed,
    )


def absorb_maybe(previous, queries, head_keys, head_vals, allowed):
    return absorb_block(previous, queries, head_keys, head_vals, allowed)


def on_device(
    x_img,
    x_txt,
    modulation,
    w_img,
    w_txt,
    w_out,
    w_final,
    lengths,
    block_mask,
    timestep,
    latent,
    conv_w,
):
    tokens = x_img[0]
    factors = modulation[0]
    tok_rows = tokens.shape[0]
    head_cols = w_out.shape[0] * lax.axis_size("req")
    head_count = head_cols // HD
    h_img = modulate(tokens, factors[0], factors[1]).astype(jnp.bfloat16)
    h_txt = modulate(x_txt[0], factors[3], factors[4]).astype(jnp.bfloat16)
    qkv = jnp.dot(
        h_img, lax.all_gather(w_img, "req", axis=1, tiled=True), preferred_element_type=jnp.float32
    ).astype(jnp.bfloat16)
    kv_txt = jnp.dot(
        h_txt, lax.all_gather(w_txt, "req", axis=1, tiled=True), preferred_element_type=jnp.float32
    ).astype(jnp.bfloat16)
    keys_txt = kv_txt[:, :head_cols].reshape(-1, head_count, HD)
    vals_txt = kv_txt[:, head_cols:].reshape(-1, head_count, HD)
    length = lengths[0]
    queries = qkv[:, :head_cols].reshape(tok_rows, head_count, HD)
    keys_img = qkv[:, head_cols : 2 * head_cols]
    vals_img = qkv[:, 2 * head_cols :]
    mask_row = block_mask[0, 0]
    tile_count = mask_row.shape[0]
    start_state = text_state(queries, keys_txt, vals_txt, length)
    piece_keys = lax.all_gather(keys_img, "blk", axis=0, tiled=True)
    piece_vals = lax.all_gather(vals_img, "blk", axis=0, tiled=True)
    piece_len = piece_keys.shape[0]
    key_tile = jnp.arange(piece_len, dtype=jnp.int32) // tok_rows
    tile_hit = key_tile[:, None] == jnp.arange(tile_count, dtype=jnp.int32)[None, :]
    allowed = jnp.sum(jnp.where(tile_hit, mask_row[None, :], 0), axis=1) == 1
    head_keys = piece_keys.reshape(piece_len, head_count, HD)
    head_vals = piece_vals.reshape(piece_len, head_count, HD)
    run_max, run_sum, run_acc = absorb_maybe(
        start_state, queries, head_keys, head_vals, allowed[None, None, :]
    )
    attended = (run_acc / run_sum[:, :, None]).reshape(tok_rows, head_cols).astype(jnp.bfloat16)
    projected = jnp.dot(
        attended,
        lax.all_gather(w_out, "req", axis=0, tiled=True),
        preferred_element_type=jnp.float32,
    )
    residual = tokens.astype(jnp.float32) + factors[2] * projected
    final_in = modulate(residual, factors[5], factors[6]).astype(jnp.bfloat16)
    token_out = jnp.dot(final_in, w_final, preferred_element_type=jnp.float32)
    velocity = unpatchify(token_out, GRIDW, PATCH, LATC)[None]
    step_index = timestep[0]
    sigma_step = sigma_of(step_index + 1, NSTEPS) - sigma_of(step_index, NSTEPS)
    latent_next = latent + sigma_step * velocity
    decoded = (latent_next / LATENT_SCALE + LATENT_SHIFT).astype(jnp.bfloat16)
    padded = with_halo(decoded, (("blk", 2),), 1)
    padded = jnp.pad(padded[0], ((0, 0), (0, 0), (1, 1)))
    features = convolve(padded, conv_w).astype(jnp.bfloat16)[None]
    return (velocity, latent_next, features)


def solution(mesh):
    return jax.shard_map(
        on_device,
        mesh=mesh,
        in_specs=(
            P("req", "blk", None),
            P("req", None, None),
            P("req", None, None),
            P(None, "req"),
            P(None, "req"),
            P("req", None),
            P(),
            P("req"),
            P("req", "blk", None),
            P("req"),
            P("req", None, "blk", None),
            P(),
        ),
        out_specs=(
            P("req", None, "blk", None),
            P("req", None, "blk", None),
            P("req", None, "blk", None),
        ),
        check_vma=False,
    )
```

profile of v0, /device:TPU:0, one launch (start us, length us, event | category | flops | bytes accessed | tf_op | source)
XLA Modules:
  0.0 230.1 jit_solution(16971153236048344387)
XLA Ops:
  8.7 0.9 add_reduce_fusion
  10.2 51.3 %all-gather.8.cloned.1.call-done = bf16[1536,2304]{0,1:T(8,128)(2,1)} async-done(((bf16[1536,288]{0,1:T(8,128)(2,1)}), bf16[1536,2304]{0,1:T(8,128)(2,1)}) %all-gather.8.cloned.1.call-update) | async-done | bytes 7077904 | tf_op jit(solution)/shard_map/all_gather | solution.py:132
  61.5 5.2 %convolution_convert_fusion = bf16[256,2304]{1,0:T(8,128)(2,1)S(1)} fusion(bf16[1536,2304]{0,1:T(8,128)(2,1)} %all-gather.8.cloned.1.call-done, bf16[1,256,1536]{2,1,0:T(8,128)(2,1)S(1)} %copy-done.2, f32[1536]{0:T(1024)S(1)} %get-tuple-element.16, f32[1536]{0:T(1024)S(1)} %get-tuple-element.17, f32[256]{0:T(256)S(1)} %add_rsqrt_fusion.1, ...), kind=kOutput, calls=%fused_computation.10 | convolution fusion | flops 1814888448 | bytes 9058304 | tf_op jit(solution)/shard_map/dot_general | solution.py:131
  66.7 1.0 fusion.69
  70.8 1.0 copy.66
  71.9 30.4 %all-gather.6.cloned.1.call-done = bf16[1536,1536]{0,1:T(8,128)(2,1)} async-done(((bf16[1536,192]{0,1:T(8,128)(2,1)}), bf16[1536,1536]{0,1:T(8,128)(2,1)}) %all-gather.6.cloned.1.call-update) | async-done | bytes 4718608 | tf_op jit(solution)/shard_map/all_gather | solution.py:135
  102.3 4.0 %convolution_convert_fusion.1 = bf16[154,1536]{1,0:T(8,128)(2,1)S(1)} fusion(bf16[1536,1536]{0,1:T(8,128)(2,1)} %all-gather.6.cloned.1.call-done, bf16[1,154,1536]{2,1,0:T(8,128)(2,1)S(1)} %copy-done.4, f32[1536]{0:T(1024)S(1)} %get-tuple-element.18, f32[1536]{0:T(1024)S(1)} %get-tuple-element.19, f32[154]{0:T(256)S(1)} %add_rsqrt_fusion.2, ...), kind=kOutput, calls=%fused_computation.13 | convolution fusion | flops 728318976 | bytes 5678288 | tf_op jit(solution)/shard_map/dot_general | solution.py:134
  106.4 0.9 copy.60
  107.3 0.9 copy.59
  108.4 1.6 bitcast_reduce_fusion.1
  110.6 30.5 %all-gather.10.cloned.1.call-done = bf16[1024,768]{1,0:T(8,128)(2,1)} async-done(((bf16[256,768]{1,0:T(8,128)(2,1)}), bf16[1024,768]{1,0:T(8,128)(2,1)}) %all-gather.10.cloned.1.call-update) | async-done | bytes 1572880 | tf_op jit(solution)/shard_map/all_gather | solution.py:146
  141.0 2.6 %copy.62 = bf16[1024,768]{0,1:T(8,128)(2,1)} copy(bf16[1024,768]{1,0:T(8,128)(2,1)} %all-gather.10.cloned.1.call-done) | data formatting | bytes 3145728 | tf_op jit(solution)/shard_map/all_gather | solution.py:146
  143.6 8.8 %bitcast_reduce_fusion = (f32[256,12]{0,1:T(8,128)S(1)}, f32[12,1024,256]{2,1,0:T(8,128)}) fusion(pred[1024]{0:T(1024)(128)(4,1)S(1)} %broadcast_compare_fusion, bf16[1024,12,64]{0,2,1:T(8,128)(2,1)} %bitcast.129, bf16[256,12,64]{0,2,1:T(8,128)(2,1)S(1)} %bitcast.134), kind=kOutput, calls=%fused_computation.1 | convolution fusion | flops 412087296 | bytes 14562304 | tf_op jit(solution)/shard_map/qhd,khd->qhk/dot_general | solution.py:89
  152.5 26.0 %all-gather.12.cloned.1.call-done = bf16[1024,768]{1,0:T(8,128)(2,1)} async-done(((bf16[256,768]{1,0:T(8,128)(2,1)}), bf16[1024,768]{1,0:T(8,128)(2,1)}) %all-gather.12.cloned.1.call-update) | async-done | bytes 1572880 | tf_op jit(solution)/shard_map/all_gather | solution.py:147
  178.4 2.6 %copy.63 = bf16[1024,768]{0,1:T(8,128)(2,1)} copy(bf16[1024,768]{1,0:T(8,128)(2,1)} %all-gather.12.cloned.1.call-done) | data formatting | bytes 3145728 | tf_op jit(solution)/shard_map/all_gather | solution.py:147
  181.0 7.2 %fusion.2 = f32[256,12]{0,1:T(8,128)S(1)} fusion(f32[12,1024,256]{2,1,0:T(8,128)} %get-tuple-element.45, f32[256,12]{0,1:T(8,128)S(1)} %max.13, pred[1024]{0:T(1024)(128)(4,1)S(1)} %broadcast_compare_fusion), kind=kLoop, calls=%fused_computation.5 | loop fusion | flops 15725568 | bytes 12608512 | tf_op jit(solution)/shard_map/reduce_sum | solution.py:101
  188.3 1.3 copy-done.1
  189.6 4.3 %fusion.20 = f32[256,12,64]{0,2,1:T(8,128)S(1)} fusion(bf16[1024,12,64]{0,2,1:T(8,128)(2,1)} %bitcast.135, f32[12,1024,256]{2,1,0:T(8,128)S(1)} %copy-done.1, f32[256,12]{0,1:T(8,128)S(1)} %max.13, pred[1024]{0:T(1024)(128)(4,1)S(1)} %broadcast_compare_fusion), kind=kOutput, calls=%fused_computation.33 | convolution fusion | flops 418381824 | bytes 14955520 | tf_op jit(solution)/shard_map/qhk,khd->qhd/dot_general | solution.py:96
  194.6 13.5 %all-gather.14.cloned.1.call-done = bf16[768,1536]{1,0:T(8,128)(2,1)} async-done(((bf16[96,1536]{1,0:T(8,128)(2,1)}), bf16[768,1536]{1,0:T(8,128)(2,1)}) %all-gather.14.cloned.1.call-update) | async-done | bytes 2359312 | tf_op jit(solution)/shard_map/all_gather | solution.py:160
  208.1 2.5 %fusion.72 = (f32[256]{0:T(256)S(1)}, f32[256,1536]{1,0:T(8,128)S(1)}) fusion(bf16[256,768]{0,1:T(8,128)(2,1)S(1)} %bitcast.137, bf16[768,1536]{1,0:T(8,128)(2,1)} %all-gather.14.cloned.1.call-done, f32[1536]{0:T(1024)S(1)} %get-tuple-element.20, bf16[1,256,1536]{2,1,0:T(8,128)(2,1)S(1)} %copy-done.2), kind=kOutput, calls=%fused_computation.127 | convolution fusion | flops 605552384 | bytes 5118976 | tf_op jit(solution)/shard_map/dot_general | solution.py:158
  212.0 3.4 %collective-permute-start = (bf16[1,16,1,128]{1,3,2,0:T(8,128)(2,1)S(1)}, bf16[1,16,1,128]{1,3,2,0:T(8,128)(2,1)S(1)}, u32[]{:S(2)}, u32[]{:S(2)}) collective-permute-start(bf16[1,16,1,128]{1,3,2,0:T(8,128)(2,1)S(1)} %get-tuple-element.31), channel_id=1, source_target_pairs={{0,1},{1,2},{2,3},{4,5},{5,6},{6,7},{8,9},{9,10},{10,11},{12,13},{... | collective-permute-start | bytes 12296 | tf_op jit(solution)/shard_map/ppermute | solution.py:24
  215.4 1.3 collective-permute-start.1
  218.5 2.7 %collective-permute-done.1 = bf16[1,16,1,128]{1,3,2,0:T(8,128)(2,1)S(1)} collective-permute-done((bf16[1,16,1,128]{1,3,2,0:T(8,128)(2,1)S(1)}, bf16[1,16,1,128]{1,3,2,0:T(8,128)(2,1)S(1)}, u32[]{:S(2)}, u32[]{:S(2)}) %collective-permute-start.1) | collective-permute-done | bytes 4128 | tf_op jit(solution)/shard_map/ppermute | solution.py:27
  222.1 1.5 copy.81
  (71 shorter events, 9.1 us)
Async XLA Ops:
  7.2 203.8 %copy-start = (bf16[1536,64]{0,1:T(8,128)(2,1)S(1)}, bf16[1536,64]{0,1:T(8,128)(2,1)}, u32[]{:S(2)}) copy-start(bf16[1536,64]{0,1:T(8,128)(2,1)} %param.18) | copy-start | bytes 589828
  7.2 2.5 %copy-start.2 = (bf16[1,256,1536]{2,1,0:T(8,128)(2,1)S(1)}, bf16[1,256,1536]{2,1,0:T(8,128)(2,1)}, u32[]{:S(2)}) copy-start(bf16[1,256,1536]{2,1,0:T(8,128)(2,1)} %param.12) | copy-start | bytes 2359300
  7.2 54.3 %all-gather.8.cloned.1.call-start = ((), (), s32[]{:S(2)}) async-start(), calls=%async_computation.1 | async-start | bytes 7962624 | tf_op jit(solution)/shard_map/all_gather | solution.py:132
  7.9 94.4 %all-gather.6.cloned.1.call-start = ((), (), s32[]{:S(2)}) async-start(), calls=%async_computation | async-start | bytes 5308416 | tf_op jit(solution)/shard_map/all_gather | solution.py:135
  8.7 132.4 %all-gather.10.cloned.1.call-start = ((), (), s32[]{:S(2)}) async-start(), calls=%async_computation.2 | async-start | bytes 1966080 | tf_op jit(solution)/shard_map/all_gather | solution.py:146
  66.7 2.9 %copy-start.4 = (bf16[1,154,1536]{2,1,0:T(8,128)(2,1)S(1)}, bf16[1,154,1536]{2,1,0:T(8,128)(2,1)}, u32[]{:S(2)}) copy-start(bf16[1,154,1536]{2,1,0:T(8,128)(2,1)} %param.13) | copy-start | bytes 1419268
  66.7 4.0 %copy-start.8 = (s32[1,1,4]{2,1,0:T(1,128)S(1)}, s32[1,1,4]{2,1,0:T(1,128)}, u32[]{:S(2)}) copy-start(s32[1,1,4]{2,1,0:T(1,128)} %param.20) | copy-start | bytes 52
  66.7 4.1 %copy-start.7 = (f32[1,16,8,128]{3,2,1,0:T(8,128)S(1)}, f32[1,16,8,128]{3,2,1,0:T(8,128)}, u32[]{:S(2)}) copy-start(f32[1,16,8,128]{3,2,1,0:T(8,128)} %param.22) | copy-start | bytes 196612
  67.7 110.8 %all-gather.12.cloned.1.call-start = ((), (), s32[]{:S(2)}) async-start(), calls=%async_computation.3 | async-start | bytes 1966080 | tf_op jit(solution)/shard_map/all_gather | solution.py:147
  68.3 139.8 %all-gather.14.cloned.1.call-start = ((), (), s32[]{:S(2)}) async-start(), calls=%async_computation.4 | async-start | bytes 2654208 | tf_op jit(solution)/shard_map/all_gather | solution.py:160
  181.0 8.5 %copy-start.1 = (f32[12,1024,256]{2,1,0:T(8,128)S(1)}, f32[12,1024,256]{2,1,0:T(8,128)}, u32[]{:S(2)}) copy-start(f32[12,1024,256]{2,1,0:T(8,128)} %get-tuple-element.45) | copy-start | bytes 37748740
  189.6 4.3 %copy-start.5 = (bf16[154,768]{0,1:T(8,128)(2,1)S(1)}, bf16[154,768]{0,1:T(8,128)(2,1)}, u32[]{:S(2)}) copy-start(bf16[154,768]{0,1:T(8,128)(2,1)} %copy.59) | copy-start | bytes 709636
  210.6 1.2 copy-start.3
  211.8 9.8 %copy-start.6 = (bf16[512,144]{0,1:T(8,128)(2,1)S(1)}, bf16[512,144]{0,1:T(8,128)(2,1)}, u32[]{:S(2)}) copy-start(bf16[512,144]{0,1:T(8,128)(2,1)} %param.23) | copy-start | bytes 442372
  212.0 6.4 %collective-permute-start = (bf16[1,16,1,128]{1,3,2,0:T(8,128)(2,1)S(1)}, bf16[1,16,1,128]{1,3,2,0:T(8,128)(2,1)S(1)}, u32[]{:S(2)}, u32[]{:S(2)}) collective-permute-start(bf16[1,16,1,128]{1,3,2,0:T(8,128)(2,1)S(1)} %get-tuple-element.31), channel_id=1, source_target_pairs={{0,1},{1,2},{2,3},{4,5},{5,6},{6,7},{8,9},{9,10},{10,11},{12,13},{... | collective-permute-start | bytes 12296 | tf_op jit(solution)/shard_map/ppermute | solution.py:24
  215.4 5.8 %collective-permute-start.1 = (bf16[1,16,1,128]{1,3,2,0:T(8,128)(2,1)S(1)}, bf16[1,16,1,128]{1,3,2,0:T(8,128)(2,1)S(1)}, u32[]{:S(2)}, u32[]{:S(2)}) collective-permute-start(bf16[1,16,1,128]{1,3,2,0:T(8,128)(2,1)S(1)} %get-tuple-element.32), channel_id=1, source_target_pairs={{1,0},{2,1},{3,2},{5,4},{6,5},{7,6},{9,8},{10,9},{11,10},{13,12},{... | collective-permute-start | bytes 12296 | tf_op jit(solution)/shard_map/ppermute | solution.py:27
Sparse Core Ops, SparseCore 0:
  9.9 51.5 all-gather.7
  63.4 38.9 all-gather.5
  103.9 37.0 all-gather.9
  142.5 35.9 all-gather.11
  180.2 27.8 all-gather.13
where the time goes:
time: 231 us; the launch traced here: 230 us
  waiting for transfers between devices  157 us (68%)
  matrix products  28 us (12%)
  between operations  15.5 us (7%)
  local copies, waits for them, and re-layouts  14.5 us (6%)
  other arithmetic  10.2 us (4%)
  starting transfers between devices  4.88 us (2%)
    all_gather x1, waiting for transfers between devices, on_device(): lax.all_gather(w_img, 'req', axis=1, tiled=True)  51.3 us
    all_gather x1, waiting for transfers between devices, on_device(): piece_keys = lax.all_gather(keys_img, 'blk', axis=0, tiled=True)  30.5 us
    all_gather x1, waiting for transfers between devices, on_device(): lax.all_gather(w_txt, 'req', axis=1, tiled=True)  30.4 us
    all_gather x1, waiting for transfers between devices, on_device(): piece_vals = lax.all_gather(vals_img, 'blk', axis=0, tiled=True)  26 us
    all_gather x1, waiting for transfers between devices, on_device(): lax.all_gather(w_out, 'req', axis=0, tiled=True)  13.5 us
    dot_general x1, matrix products, absorb_block(): jnp.einsum('qhd,khd->qhk', queries, head_keys, preferred_element_type=jnp...  8.82 us
    reduce_sum x1, other arithmetic, absorb_block(): jnp.sum(weights, axis=2)  7.21 us
    unnamed x30, local copies, waits for them, and re-layouts  5.57 us
  transfers between devices with their start and end apart: 7, of which 6 were waited for; matrix products, arithmetic and copies ran while one was open for 20% of the time, Pallas kernels for 0%

commit v1 on v0

--- a/solution.py
+++ b/solution.py
@@ -14,6 +14,16 @@
 LATENT_SHIFT = 0.0609
 NEG_LARGE = -1e30
 SCORE_SCALE = 0.125
+
+
+def around_the_ring(block, axis, dim):
+    peers = lax.axis_size(axis)
+    held, blocks = (block, [block])
+    for _ in range(peers - 1):
+        held = lax.ppermute(held, axis, [(i, (i + 1) % peers) for i in range(peers)])
+        blocks.insert(0, held)
+    line = jnp.concatenate(blocks, axis=dim)
+    return jnp.roll(line, (lax.axis_index(axis) + 1) * block.shape[dim], axis=dim)
 
 
 def with_halo(block, sides, width):
@@ -144,7 +154,7 @@
     tile_count = mask_row.shape[0]
     start_state = text_state(queries, keys_txt, vals_txt, length)
     piece_keys = lax.all_gather(keys_img, "blk", axis=0, tiled=True)
-    piece_vals = lax.all_gather(vals_img, "blk", axis=0, tiled=True)
+    piece_vals = around_the_ring(vals_img, "blk", 0)
     piece_len = piece_keys.shape[0]
     key_tile = jnp.arange(piece_len, dtype=jnp.int32) // tok_rows
     tile_hit = key_tile[:, None] == jnp.arange(tile_count, dtype=jnp.int32)[None, :]

time: 231 us -> 192 us (0.83)
  waiting for transfers between devices: 157 us -> 123 us
  matrix products: 28 us -> 22.2 us
  other arithmetic: 10.2 us -> 6.64 us
  starting transfers between devices: 4.88 us -> 7.72 us
    ppermute x0 -> x3, waiting for transfers between devices: none -> 35.2 us  [around_the_ring(): lax.ppermute(held, axis, [(i, (i + 1) % peers) for i in range(peers)])]
    all_gather x1, waiting for transfers between devices: 30.4 us -> 0.02 us  [on_device(): lax.all_gather(w_txt, 'req', axis=1, tiled=True)]
    all_gather x1 -> x0, waiting for transfers between devices: 26 us -> none  [on_device(): piece_vals = lax.all_gather(vals_img, 'blk', axis=0, tiled=True)]
    all_gather x1, waiting for transfers between devices: 30.5 us -> 19.6 us  [on_device(): piece_keys = lax.all_gather(keys_img, 'blk', axis=0, tiled=True)]
    dot_general x1, matrix products: 8.82 us -> 4.23 us  [absorb_block(): jnp.einsum('qhd,khd->qhk', queries, head_keys, preferred_element_type=jnp...]
    reduce_sum x1, other arithmetic: 7.21 us -> 3.62 us  [absorb_block(): jnp.sum(weights, axis=2)]
    dynamic_slice x0 -> x2, local copies, waits for them, and re-layouts: none -> 3.16 us  [around_the_ring(): jnp.roll(line, (lax.axis_index(axis) + 1) * block.shape[dim], axis=dim)]
    ppermute x1, waiting for transfers between devices: 2.72 us -> 0.01 us  [with_halo(): lax.ppermute(lax.slice_in_dim(block, 0, width, axis=dim), axis, backward)]
  transfers between devices with their start and end apart: 7 -> 9, of which waited for: 6 -> 6; matrix products, arithmetic and copies ran while one was open for 20% -> 19% of each run, Pallas kernels for 0% -> 0%
where the time goes in v1:
time: 192 us; the launch traced here: 191 us
  waiting for transfers between devices  123 us (64%)
  matrix products  22.2 us (12%)
  local copies, waits for them, and re-layouts  15.6 us (8%)
  between operations  15.6 us (8%)
  starting transfers between devices  7.72 us (4%)
  other arithmetic  6.64 us (3%)
    all_gather x1, waiting for transfers between devices, on_device(): lax.all_gather(w_img, 'req', axis=1, tiled=True)  51.3 us
    ppermute x3, waiting for transfers between devices, around_the_ring(): lax.ppermute(held, axis, [(i, (i + 1) % peers) for i in range(peers)])  35.2 us
    all_gather x1, waiting for transfers between devices, on_device(): piece_keys = lax.all_gather(keys_img, 'blk', axis=0, tiled=True)  19.6 us
    all_gather x1, waiting for transfers between devices, on_device(): lax.all_gather(w_out, 'req', axis=0, tiled=True)  15.6 us
    unnamed x39, local copies, waits for them, and re-layouts  6.14 us
    dot_general x1, matrix products, on_device(): jnp.dot(h_img, lax.all_gather(w_img, 'req', axis=1, tiled=True), preferre...  5.16 us
    ppermute x1, starting transfers between devices, with_halo(): lax.ppermute(lax.slice_in_dim(block, block.shape[dim] - width, None, axis...  4.55 us
    dot_general x1, matrix products, on_device(): jnp.dot(h_txt, lax.all_gather(w_txt, 'req', axis=1, tiled=True), preferre...  4.25 us
  transfers between devices with their start and end apart: 9, of which 6 were waited for; matrix products, arithmetic and copies ran while one was open for 19% of the time, Pallas kernels for 0%

profile of v1, /device:TPU:0, one launch (start us, length us, event | category | flops | bytes accessed | tf_op | source)
XLA Modules:
  0.0 191.2 jit_solution(7897881443088850206)
XLA Ops:
  10.2 51.3 %all-gather.7.cloned.1.call-done = bf16[1536,2304]{0,1:T(8,128)(2,1)} async-done(((bf16[1536,288]{0,1:T(8,128)(2,1)}), bf16[1536,2304]{0,1:T(8,128)(2,1)}) %all-gather.7.cloned.1.call-update) | async-done | bytes 7077904 | tf_op jit(solution)/shard_map/all_gather | solution.py:142
  61.5 5.2 %convolution_convert_fusion = bf16[256,2304]{1,0:T(8,128)(2,1)S(1)} fusion(bf16[1536,2304]{0,1:T(8,128)(2,1)} %all-gather.7.cloned.1.call-done, bf16[1,256,1536]{2,1,0:T(8,128)(2,1)S(1)} %copy-done.1, f32[1536]{0:T(1024)S(1)} %get-tuple-element.16, f32[1536]{0:T(1024)S(1)} %get-tuple-element.17, f32[256]{0:T(256)S(1)} %add_rsqrt_fusion.1, ...), kind=kOutput, calls=%fused_computation.10 | convolution fusion | flops 1814888448 | bytes 9058304 | tf_op jit(solution)/shard_map/dot_general | solution.py:141
  66.7 1.5 collective-permute-start
  68.2 11.6 %collective-permute-done = bf16[256,768]{1,0:T(8,128)(2,1)S(1)} collective-permute-done((bf16[256,768]{1,0:T(8,128)(2,1)S(1)}, bf16[256,768]{1,0:T(8,128)(2,1)S(1)}, u32[]{:S(2)}, u32[]{:S(2)}) %collective-permute-start) | collective-permute-done | bytes 393248 | tf_op jit(solution)/shard_map/ppermute | solution.py:23
  79.8 12.3 %collective-permute-done.1 = bf16[256,768]{1,0:T(8,128)(2,1)S(1)} collective-permute-done((bf16[256,768]{1,0:T(8,128)(2,1)S(1)}, bf16[256,768]{1,0:T(8,128)(2,1)S(1)}, u32[]{:S(2)}, u32[]{:S(2)}) %collective-permute-start.1) | collective-permute-done | bytes 393248 | tf_op jit(solution)/shard_map/ppermute | solution.py:23
  92.1 11.3 %collective-permute-done.2 = bf16[256,768]{1,0:T(8,128)(2,1)S(1)} collective-permute-done((bf16[256,768]{1,0:T(8,128)(2,1)S(1)}, bf16[256,768]{1,0:T(8,128)(2,1)S(1)}, u32[]{:S(2)}, u32[]{:S(2)}) %collective-permute-start.2) | collective-permute-done | bytes 393248 | tf_op jit(solution)/shard_map/ppermute | solution.py:23
  104.5 1.7 copy-done.5
  108.7 1.0 copy.65
  109.9 4.3 %convolution_convert_fusion.1 = bf16[154,1536]{1,0:T(8,128)(2,1)S(1)} fusion(bf16[1536,1536]{0,1:T(8,128)(2,1)} %all-gather.5.cloned.1.call-done, bf16[1,154,1536]{2,1,0:T(8,128)(2,1)S(1)} %copy-done.3, f32[1536]{0:T(1024)S(1)} %get-tuple-element.18, f32[1536]{0:T(1024)S(1)} %get-tuple-element.19, f32[154]{0:T(256)S(1)} %add_rsqrt_fusion.2, ...), kind=kOutput, calls=%fused_computation.13 | convolution fusion | flops 728318976 | bytes 5678288 | tf_op jit(solution)/shard_map/dot_general | solution.py:144
  114.2 0.9 copy.59
  115.1 0.9 copy.58
  116.0 1.5 constant_dynamic-slice_fusion
  117.5 1.7 copy.62
  119.3 1.6 bitcast_reduce_fusion.1
  121.5 19.6 %all-gather.9.cloned.1.call-done = bf16[1024,768]{1,0:T(8,128)(2,1)} async-done(((bf16[256,768]{1,0:T(8,128)(2,1)}), bf16[1024,768]{1,0:T(8,128)(2,1)}) %all-gather.9.cloned.1.call-update) | async-done | bytes 1572880 | tf_op jit(solution)/shard_map/all_gather | solution.py:156
  141.0 2.6 %copy.61 = bf16[1024,768]{0,1:T(8,128)(2,1)} copy(bf16[1024,768]{1,0:T(8,128)(2,1)} %all-gather.9.cloned.1.call-done) | data formatting | bytes 3145728 | tf_op jit(solution)/shard_map/all_gather | solution.py:156
  143.6 4.2 %bitcast_reduce_fusion = (f32[256,12]{0,1:T(8,128)S(1)}, f32[12,1024,256]{2,1,0:T(8,128)S(1)}) fusion(pred[1024]{0:T(1024)(128)(4,1)S(1)} %broadcast_compare_fusion, bf16[1024,12,64]{0,2,1:T(8,128)(2,1)} %bitcast.129, bf16[256,12,64]{0,2,1:T(8,128)(2,1)S(1)} %bitcast.134), kind=kOutput, calls=%fused_computation.1 | convolution fusion | flops 412087296 | bytes 14562304 | tf_op jit(solution)/shard_map/qhd,khd->qhk/dot_general | solution.py:99
  147.9 3.6 %fusion.2 = f32[256,12]{0,1:T(8,128)S(1)} fusion(f32[12,1024,256]{2,1,0:T(8,128)S(1)} %get-tuple-element.45, f32[256,12]{0,1:T(8,128)S(1)} %max.13, pred[1024]{0:T(1024)(128)(4,1)S(1)} %broadcast_compare_fusion), kind=kLoop, calls=%fused_computation.5 | loop fusion | flops 15725568 | bytes 12608512 | tf_op jit(solution)/shard_map/reduce_sum | solution.py:111
  151.6 2.8 %fusion.20 = f32[256,12,64]{0,2,1:T(8,128)S(1)} fusion(bf16[1024,12,64]{0,2,1:T(8,128)(2,1)S(1)} %bitcast.135, f32[12,1024,256]{2,1,0:T(8,128)S(1)} %get-tuple-element.45, f32[256,12]{0,1:T(8,128)S(1)} %max.13, pred[1024]{0:T(1024)(128)(4,1)S(1)} %broadcast_compare_fusion), kind=kOutput, calls=%fused_computation.33 | convolution fusion | flops 418381824 | bytes 14955520 | tf_op jit(solution)/shard_map/qhk,khd->qhd/dot_general | solution.py:106
  155.1 15.6 %all-gather.11.cloned.1.call-done = bf16[768,1536]{1,0:T(8,128)(2,1)} async-done(((bf16[96,1536]{1,0:T(8,128)(2,1)}), bf16[768,1536]{1,0:T(8,128)(2,1)}) %all-gather.11.cloned.1.call-update) | async-done | bytes 2359312 | tf_op jit(solution)/shard_map/all_gather | solution.py:170
  170.7 2.5 %fusion.72 = (f32[256]{0:T(256)S(1)}, f32[256,1536]{1,0:T(8,128)S(1)}) fusion(bf16[256,768]{0,1:T(8,128)(2,1)S(1)} %bitcast.137, bf16[768,1536]{1,0:T(8,128)(2,1)} %all-gather.11.cloned.1.call-done, f32[1536]{0:T(1024)S(1)} %get-tuple-element.20, bf16[1,256,1536]{2,1,0:T(8,128)(2,1)S(1)} %copy-done.1), kind=kOutput, calls=%fused_computation.136 | convolution fusion | flops 605552384 | bytes 5118976 | tf_op jit(solution)/shard_map/dot_general | solution.py:168
  174.6 1.3 collective-permute-start.4
  175.9 4.5 %collective-permute-start.3 = (bf16[1,16,1,128]{1,3,2,0:T(8,128)(2,1)S(1)}, bf16[1,16,1,128]{1,3,2,0:T(8,128)(2,1)S(1)}, u32[]{:S(2)}, u32[]{:S(2)}) collective-permute-start(bf16[1,16,1,128]{1,3,2,0:T(8,128)(2,1)S(1)} %get-tuple-element.31), channel_id=1, source_target_pairs={{0,1},{1,2},{2,3},{4,5},{5,6},{6,7},{8,9},{9,10},{10,11},{12,13},{... | collective-permute-start | bytes 12296 | tf_op jit(solution)/shard_map/ppermute | solution.py:34
  183.2 1.5 copy.80
  (85 shorter events, 10.6 us)
Async XLA Ops:
  7.2 166.4 %copy-start = (bf16[1536,64]{0,1:T(8,128)(2,1)S(1)}, bf16[1536,64]{0,1:T(8,128)(2,1)}, u32[]{:S(2)}) copy-start(bf16[1536,64]{0,1:T(8,128)(2,1)} %param.18) | copy-start | bytes 589828
  7.2 2.5 %copy-start.1 = (bf16[1,256,1536]{2,1,0:T(8,128)(2,1)S(1)}, bf16[1,256,1536]{2,1,0:T(8,128)(2,1)}, u32[]{:S(2)}) copy-start(bf16[1,256,1536]{2,1,0:T(8,128)(2,1)} %param.12) | copy-start | bytes 2359300
  7.2 54.3 %all-gather.7.cloned.1.call-start = ((), (), s32[]{:S(2)}) async-start(), calls=%async_computation.1 | async-start | bytes 7962624 | tf_op jit(solution)/shard_map/all_gather | solution.py:142
  7.9 101.9 %all-gather.5.cloned.1.call-start = ((), (), s32[]{:S(2)}) async-start(), calls=%async_computation | async-start | bytes 5308416 | tf_op jit(solution)/shard_map/all_gather | solution.py:145
  8.7 132.4 %all-gather.9.cloned.1.call-start = ((), (), s32[]{:S(2)}) async-start(), calls=%async_computation.2 | async-start | bytes 1966080 | tf_op jit(solution)/shard_map/all_gather | solution.py:156
  66.7 13.1 %collective-permute-start = (bf16[256,768]{1,0:T(8,128)(2,1)S(1)}, bf16[256,768]{1,0:T(8,128)(2,1)S(1)}, u32[]{:S(2)}, u32[]{:S(2)}) collective-permute-start(bf16[256,768]{1,0:T(8,128)(2,1)S(1)} %slice.106), channel_id=1, source_target_pairs={{0,1},{1,2},{2,3},{3,0},{4,5},{5,6},{6,7},{7,4},{8,9},{9,10},{10,1... | collective-permute-start | bytes 1179656 | tf_op jit(solution)/shard_map/ppermute | solution.py:23
  79.8 12.3 %collective-permute-start.1 = (bf16[256,768]{1,0:T(8,128)(2,1)S(1)}, bf16[256,768]{1,0:T(8,128)(2,1)S(1)}, u32[]{:S(2)}, u32[]{:S(2)}) collective-permute-start(bf16[256,768]{1,0:T(8,128)(2,1)S(1)} %collective-permute-done), channel_id=1, source_target_pairs={{0,1},{1,2},{2,3},{3,0},{4,5},{5,6},{6,7},{7,4},{8,9},{9,10},{10,1... | collective-permute-start | bytes 1179656 | tf_op jit(solution)/shard_map/ppermute | solution.py:23
  92.1 11.3 %collective-permute-start.2 = (bf16[256,768]{1,0:T(8,128)(2,1)S(1)}, bf16[256,768]{1,0:T(8,128)(2,1)S(1)}, u32[]{:S(2)}, u32[]{:S(2)}) collective-permute-start(bf16[256,768]{1,0:T(8,128)(2,1)S(1)} %collective-permute-done.1), channel_id=1, source_target_pairs={{0,1},{1,2},{2,3},{3,0},{4,5},{5,6},{6,7},{7,4},{8,9},{9,10},{10,1... | collective-permute-start | bytes 1179656 | tf_op jit(solution)/shard_map/ppermute | solution.py:23
  103.6 3.9 %copy-start.9 = (s32[1,1,4]{2,1,0:T(1,128)S(1)}, s32[1,1,4]{2,1,0:T(1,128)}, u32[]{:S(2)}) copy-start(s32[1,1,4]{2,1,0:T(1,128)} %param.20) | copy-start | bytes 52
  103.7 4.6 %copy-start.3 = (bf16[1,154,1536]{2,1,0:T(8,128)(2,1)S(1)}, bf16[1,154,1536]{2,1,0:T(8,128)(2,1)}, u32[]{:S(2)}) copy-start(bf16[1,154,1536]{2,1,0:T(8,128)(2,1)} %param.13) | copy-start | bytes 1419268
  103.7 5.0 %copy-start.8 = (f32[1,16,8,128]{3,2,1,0:T(8,128)S(1)}, f32[1,16,8,128]{3,2,1,0:T(8,128)}, u32[]{:S(2)}) copy-start(f32[1,16,8,128]{3,2,1,0:T(8,128)} %param.22) | copy-start | bytes 196612
  104.5 1.7 copy-start.5
  106.2 64.5 %all-gather.11.cloned.1.call-start = ((), (), s32[]{:S(2)}) async-start(), calls=%async_computation.3 | async-start | bytes 2654208 | tf_op jit(solution)/shard_map/all_gather | solution.py:170
  147.9 3.7 %copy-start.4 = (bf16[1024,768]{0,1:T(8,128)(2,1)S(1)}, bf16[1024,768]{0,1:T(8,128)(2,1)}, u32[]{:S(2)}) copy-start(bf16[1024,768]{0,1:T(8,128)(2,1)} %copy.62) | copy-start | bytes 4718596
  151.6 2.8 %copy-start.6 = (bf16[154,768]{0,1:T(8,128)(2,1)S(1)}, bf16[154,768]{0,1:T(8,128)(2,1)}, u32[]{:S(2)}) copy-start(bf16[154,768]{0,1:T(8,128)(2,1)} %copy.58) | copy-start | bytes 709636
  173.2 1.2 copy-start.2
  174.5 8.3 %copy-start.7 = (bf16[512,144]{0,1:T(8,128)(2,1)S(1)}, bf16[512,144]{0,1:T(8,128)(2,1)}, u32[]{:S(2)}) copy-start(bf16[512,144]{0,1:T(8,128)(2,1)} %param.23) | copy-start | bytes 442372
  174.6 7.6 %collective-permute-start.4 = (bf16[1,16,1,128]{1,3,2,0:T(8,128)(2,1)S(1)}, bf16[1,16,1,128]{1,3,2,0:T(8,128)(2,1)S(1)}, u32[]{:S(2)}, u32[]{:S(2)}) collective-permute-start(bf16[1,16,1,128]{1,3,2,0:T(8,128)(2,1)S(1)} %get-tuple-element.32), channel_id=1, source_target_pairs={{1,0},{2,1},{3,2},{5,4},{6,5},{7,6},{9,8},{10,9},{11,10},{13,12},{... | collective-permute-start | bytes 12296 | tf_op jit(solution)/shard_map/ppermute | solution.py:37
  175.9 6.3 %collective-permute-start.3 = (bf16[1,16,1,128]{1,3,2,0:T(8,128)(2,1)S(1)}, bf16[1,16,1,128]{1,3,2,0:T(8,128)(2,1)S(1)}, u32[]{:S(2)}, u32[]{:S(2)}) collective-permute-start(bf16[1,16,1,128]{1,3,2,0:T(8,128)(2,1)S(1)} %get-tuple-element.31), channel_id=1, source_target_pairs={{0,1},{1,2},{2,3},{4,5},{5,6},{6,7},{8,9},{9,10},{10,11},{12,13},{... | collective-permute-start | bytes 12296 | tf_op jit(solution)/shard_map/ppermute | solution.py:34
Sparse Core Ops, SparseCore 0:
  9.9 51.5 all-gather.6
  63.4 38.9 all-gather.4
  106.3 34.6 all-gather.8
  142.8 27.8 all-gather.10
